TPU v7x, 32 devices: a whole 2x2x4 slice. The times are simulated.
32 devices in a mesh: fsdp: 8 (over y, x, core), tp: 4 (over z).
Axes of the slice: x: 2, y: 2, z: 4, core: 2. Of those that a mesh axis runs over, the one named last changes fastest.
Arguments:
- tokens: bfloat16 [16, 1024, 1024], P('fsdp', 'tp'), may hold values from -6 to 6
- lengths: int32 [16], replicated, may hold values from 1 to 1024, 10240 in all
- perm: int32 [16], replicated, may hold values from 0 to 15, as said below
- cotangent: bfloat16 [16, 1024, 1024], P('fsdp', 'tp'), may hold values from -6 to 6
- norm1_gain: float32 [1024], replicated, may hold values from 0.5 to 1.5
- input_weight: bfloat16 [1024, 8, 771], P('fsdp', 'tp'), may hold values from -0.1875 to 0.1875
- conv_w: float32 [8, 640, 4], replicated, may hold values from -3 to 3
- decay_log: float32 [8], replicated, may hold values from -7 to -2
- decay_bias: float32 [8], replicated, may hold values from -1 to 1
- out_gain: float32 [128], replicated, may hold values from 0.5 to 1.5
- w_out: bfloat16 [1024, 1024], P('tp', 'fsdp'), may hold values from -0.1875 to 0.1875
- norm2_gain: float32 [1024], replicated, may hold values from 0.5 to 1.5
- gate_up_weight: bfloat16 [1024, 2, 2816], P('fsdp', None, 'tp'), may hold values from -0.1875 to 0.1875
- down_weight: bfloat16 [2816, 1024], P('tp', 'fsdp'), may hold values from -0.109375 to 0.109375
Outputs:
- output: bfloat16 [16, 1024, 1024], P('fsdp', 'tp')
- input_grad: bfloat16 [16, 1024, 1024], P('fsdp', 'tp')
- grad_norm1_gain: float32 [1024], replicated
- grad_w_in: float32 [1024, 8, 771], P('fsdp', 'tp')
- grad_conv_w: float32 [8, 640, 4], replicated
- grad_decay_log: float32 [8], replicated
- grad_decay_bias: float32 [8], replicated
- grad_out_gain: float32 [128], replicated
- grad_w_out: float32 [1024, 1024], P('tp', 'fsdp')
- grad_norm2_gain: float32 [1024], replicated
- grad_w_gate_up: float32 [1024, 2, 2816], P('fsdp', None, 'tp')
- grad_w_down: float32 [2816, 1024], P('tp', 'fsdp')
Inputs may be any that keep to these rules, and one draw needn't show every extreme that they name: lengths[i] is the number of live tokens of sequence i; one sequence has exactly 1024. perm is a permutation; slot d belongs to index d // 2 of fsdp. The sequences of one index of fsdp (given order) go to 2 different indices, and each index receives at most one sequence from each index.
All inputs are finite; a program needn't handle non-finite values.
Results may differ from a plain program's by a relative error of at most 0.03.
Values may be sent and summed in bfloat16 or wider, within the bound.
No kernel may reach another device: no remote copies, remote signals or barrier semaphores. Data moves between devices by JAX's collectives and lax.ppermute only.
A program may use at most 320 MiB of HBM per device.

v0:
```python
import jax
import jax.numpy as jnp
from jax import lax
from jax.sharding import PartitionSpec as P

HEAD_DIM = 128
NH = 2
SPAN = 64
EPS_NORM = 1e-05
EPS_UNIT = 1e-06
PRECISION_MAX = lax.Precision.HIGHEST


def rms_scale(value, gain):
    return value * lax.rsqrt(jnp.mean(value * value, axis=-1, keepdims=True) + EPS_NORM) * gain


def unit_norm(value):
    return value * lax.rsqrt(jnp.sum(value * value, axis=-1, keepdims=True) + EPS_UNIT)


def causal_conv(raw_values, kernel):
    kernel_len = kernel.shape[-1]
    seq_len = raw_values.shape[1]
    padded = jnp.pad(raw_values, ((0, 0), (kernel_len - 1, 0), (0, 0), (0, 0)))
    summed = jnp.zeros_like(raw_values)
    for offset in range(kernel_len):
        summed = summed + padded[:, offset : offset + seq_len] * kernel[:, :, offset]
    return summed


def carry_step(state, pieces):
    weighted_block, value_block, key_block, decay_block = pieces
    updates = value_block - jnp.einsum("shid,shdv->shiv", key_block, state, precision=PRECISION_MAX)
    carried = decay_block * state + jnp.einsum(
        "shjd,shjv->shdv", weighted_block, updates, precision=PRECISION_MAX
    )
    return (carried, (state, updates))


def delta_product(queries, key_rows, values, beta_rows, log_decay):
    batch_seqs, seq_len, head_count, head_dim = queries.shape
    value_dim = values.shape[-1]
    blocks = seq_len // SPAN
    sub_decay = jnp.concatenate([log_decay[..., None], jnp.zeros_like(beta_rows[..., 1:])], axis=-1)

    def split_steps(value):
        tail_dims = value.shape[4:]
        shaped = value.reshape((batch_seqs, blocks, SPAN, head_count, NH) + tail_dims)
        axes_order = (1, 0, 3, 2, 4) + tuple(range(5, 5 + len(tail_dims)))
        return shaped.transpose(axes_order).reshape(
            (blocks, batch_seqs, head_count, SPAN * NH) + tail_dims
        )

    block_queries = queries.reshape(batch_seqs, blocks, SPAN, head_count, head_dim).transpose(
        1, 0, 3, 2, 4
    )
    block_keys = split_steps(key_rows)
    block_values = split_steps(values)
    block_betas = split_steps(beta_rows)
    cumulative = jnp.cumsum(split_steps(sub_decay), axis=-1)
    steps_in = SPAN * NH
    row_ids = lax.broadcasted_iota(jnp.int32, (steps_in, steps_in), 0)
    col_ids = lax.broadcasted_iota(jnp.int32, (steps_in, steps_in), 1)
    strictly = col_ids < row_ids
    key_inner = jnp.einsum("nshid,nshjd->nshij", block_keys, block_keys, precision=PRECISION_MAX)
    spread_log = cumulative[..., :, None] - cumulative[..., None, :]
    fading = jnp.where(strictly, jnp.exp(jnp.where(strictly, spread_log, 0.0)), 0.0)
    lower_mat = key_inner * fading * block_betas[..., :, None]
    right_sides = jnp.concatenate(
        [
            block_betas[..., None] * block_values,
            (block_betas * jnp.exp(cumulative))[..., None] * block_keys,
        ],
        axis=-1,
    )
    solved = jax.scipy.linalg.solve_triangular(
        lower_mat, right_sides, lower=True, unit_diagonal=True
    )
    value_part = solved[..., :value_dim]
    key_part = solved[..., value_dim:]
    last_log = cumulative[..., -1:]
    weighted = block_keys * jnp.exp(last_log - cumulative)[..., None]
    block_decay = jnp.exp(last_log)[..., None]
    first_state = jnp.zeros((batch_seqs, head_count, head_dim, value_dim), jnp.float32)
    last_state, (entering, updates) = lax.scan(
        carry_step, first_state, (weighted, value_part, key_part, block_decay)
    )
    read_log = cumulative[..., NH - 1 :: NH]
    out_rows = lax.broadcasted_iota(jnp.int32, (SPAN, steps_in), 0)
    out_cols = lax.broadcasted_iota(jnp.int32, (SPAN, steps_in), 1)
    visible = out_cols <= out_rows * NH + NH - 1
    query_key = jnp.einsum("nshid,nshjd->nshij", block_queries, block_keys, precision=PRECISION_MAX)
    read_spread = read_log[..., :, None] - cumulative[..., None, :]
    read_fade = jnp.where(visible, jnp.exp(jnp.where(visible, read_spread, 0.0)), 0.0)
    from_state = jnp.einsum("nshid,nshdv->nshiv", block_queries, entering, precision=PRECISION_MAX)
    outputs = jnp.exp(read_log)[..., None] * from_state + jnp.einsum(
        "nshij,nshjv->nshiv", query_key * read_fade, updates, precision=PRECISION_MAX
    )
    return outputs.transpose(1, 0, 3, 2, 4).reshape(batch_seqs, seq_len, head_count, value_dim)


def mixer_inner(projected_rows, conv_part, log_part, bias_part, out_gain):
    batch_seqs, seq_len, head_count, _ = projected_rows.shape
    conv_ch = conv_part.shape[1]
    conv_out = jax.nn.silu(causal_conv(projected_rows[..., :conv_ch], conv_part))
    queries = unit_norm(conv_out[..., :HEAD_DIM])
    key_rows = unit_norm(
        conv_out[..., HEAD_DIM : HEAD_DIM * (1 + NH)].reshape(
            batch_seqs, seq_len, head_count, NH, HEAD_DIM
        )
    )
    values = conv_out[..., HEAD_DIM * (1 + NH) :].reshape(
        batch_seqs, seq_len, head_count, NH, HEAD_DIM
    )
    out_gate = projected_rows[..., conv_ch : conv_ch + HEAD_DIM]
    beta_rows = jax.nn.sigmoid(projected_rows[..., conv_ch + HEAD_DIM : conv_ch + HEAD_DIM + NH])
    log_decay = -jnp.exp(log_part) * jax.nn.softplus(
        projected_rows[..., conv_ch + HEAD_DIM + NH] + bias_part
    )
    result = delta_product(queries, key_rows, values, beta_rows, log_decay)
    return rms_scale(result, out_gain) * jax.nn.silu(out_gate)


def swiglu(gate_up_result):
    return jax.nn.silu(gate_up_result[..., 0, :]) * gate_up_result[..., 1, :]


def spread(value):
    return lax.all_gather(value, "tp", axis=1, tiled=True)


def collect(value):
    return lax.psum_scatter(
        value.astype(jnp.bfloat16), "tp", scatter_dimension=1, tiled=True
    ).astype(jnp.float32)


def spread_back(value):
    return lax.all_gather(value, "tp", axis=1, tiled=True)


def collect_back(value):
    return lax.psum_scatter(
        value.astype(jnp.bfloat16), "tp", scatter_dimension=1, tiled=True
    ).astype(jnp.float32)


def local(
    tokens,
    lengths,
    perm,
    cotangent,
    norm1_gain,
    input_weight,
    conv_w,
    decay_log,
    decay_bias,
    out_gain,
    w_out,
    norm2_gain,
    gate_up_weight,
    down_weight,
):
    group_count = lax.axis_size("fsdp")
    own_group = lax.axis_index("fsdp")
    tensor_pos = lax.axis_index("tp")
    slot_count = tokens.shape[0]
    piece_len = tokens.shape[1]
    sources = perm.reshape(group_count, slot_count)
    local_ids = jnp.arange(slot_count, dtype=jnp.int32)
    group_ids = jnp.arange(group_count, dtype=jnp.int32)
    from_here = sources // slot_count == own_group
    matches = jnp.logical_and(
        from_here[:, :, None], (sources % slot_count)[:, :, None] == local_ids[None, None, :]
    )
    send_pick = jnp.sum(matches.astype(jnp.int32), axis=1).astype(jnp.bfloat16)
    sending = jnp.einsum(
        "gj,jtd->gtd", send_pick, tokens, preferred_element_type=jnp.float32
    ).astype(jnp.bfloat16)
    arrived = lax.all_to_all(sending, "fsdp", split_axis=0, concat_axis=0, tiled=True)
    my_sources = lax.dynamic_index_in_dim(sources, own_group, 0, keepdims=False)
    take_pick = ((my_sources // slot_count)[:, None] == group_ids[None, :]).astype(jnp.bfloat16)
    slot_tokens = jnp.einsum("sg,gtd->std", take_pick, arrived, preferred_element_type=jnp.float32)
    slot_len = jnp.take(lengths, my_sources)
    positions = tensor_pos * piece_len + jnp.arange(piece_len, dtype=jnp.int32)
    live_mask = (positions[None, :] < slot_len[:, None]).astype(jnp.float32)[..., None]
    head_count = input_weight.shape[1]
    head_start = tensor_pos * head_count
    conv_part = lax.dynamic_slice_in_dim(conv_w, head_start, head_count, 0)
    log_part = lax.dynamic_slice_in_dim(decay_log, head_start, head_count, 0)
    bias_part = lax.dynamic_slice_in_dim(decay_bias, head_start, head_count, 0)
    input_weight_whole, out_full = (
        lax.all_gather(input_weight, "fsdp", axis=0, tiled=True),
        lax.all_gather(w_out, "fsdp", axis=1, tiled=True),
    )
    model_dim = input_weight_whole.shape[0]
    output_matrix = out_full.reshape(head_count, HEAD_DIM, model_dim)
    normed_one = rms_scale(slot_tokens, norm1_gain).astype(jnp.bfloat16)
    gathered_first = spread(normed_one)
    projected_rows = jnp.einsum(
        "mzk,kin->mzin", gathered_first, input_weight_whole, preferred_element_type=jnp.float32
    )
    gated, inner_pull = jax.vjp(
        mixer_inner, projected_rows, conv_part, log_part, bias_part, out_gain
    )
    gated_reduced = gated.astype(jnp.bfloat16)
    mixer_result = jnp.einsum(
        "gtpo,poz->gtz", gated_reduced, output_matrix, preferred_element_type=jnp.float32
    )
    middle = slot_tokens + collect(mixer_result)
    gate_up_weight_whole, down_weight_whole = (
        lax.all_gather(gate_up_weight, "fsdp", axis=0, tiled=True),
        lax.all_gather(down_weight, "fsdp", axis=1, tiled=True),
    )
    normed_two = rms_scale(middle, norm2_gain).astype(jnp.bfloat16)
    gathered_second = spread(normed_two)
    gate_up_result = jnp.einsum(
        "tux,xeg->tueg", gathered_second, gate_up_weight_whole, preferred_element_type=jnp.float32
    )
    hidden_val, hidden_pull = jax.vjp(swiglu, gate_up_result)
    hidden_reduced = hidden_val.astype(jnp.bfloat16)
    forward_net_output = jnp.einsum(
        "wqh,hv->wqv", hidden_reduced, down_weight_whole, preferred_element_type=jnp.float32
    )
    block_out = live_mask * (middle + collect(forward_net_output))
    slot_cot = live_mask * cotangent.astype(jnp.float32)
    gradient_rows_second = spread_back(slot_cot.astype(jnp.bfloat16))
    grad_down = jnp.einsum(
        "kob,koi->bi", hidden_reduced, gradient_rows_second, preferred_element_type=jnp.float32
    )
    grad_hidden = jnp.einsum(
        "igx,bx->igb", gradient_rows_second, down_weight_whole, preferred_element_type=jnp.float32
    )
    gradient_couple = hidden_pull(grad_hidden)[0]
    grad_gate_up = jnp.einsum(
        "rzt,rzih->tih",
        gathered_second.astype(jnp.float32),
        gradient_couple,
        precision=PRECISION_MAX,
    )
    grad_normed_two = jnp.einsum(
        "uxmw,zmw->uxz",
        gradient_couple,
        gate_up_weight_whole.astype(jnp.float32),
        precision=PRECISION_MAX,
    )
    norm_pull_two = jax.vjp(rms_scale, middle, norm2_gain)[1]
    grad_mid_norm, grad_gain_two = norm_pull_two(collect_back(grad_normed_two))
    grad_middle = slot_cot + grad_mid_norm
    gradient_rows_first = spread_back(grad_middle.astype(jnp.bfloat16))
    grad_out = jnp.einsum(
        "irpy,irk->pyk", gated_reduced, gradient_rows_first, preferred_element_type=jnp.float32
    ).reshape(head_count * HEAD_DIM, model_dim)
    grad_gated = jnp.einsum(
        "ein,wcn->eiwc", gradient_rows_first, output_matrix, preferred_element_type=jnp.float32
    )
    gradient_projected, grad_conv, grad_log, grad_bias, grad_gain_out = inner_pull(grad_gated)
    grad_in = jnp.einsum(
        "bwg,bwfi->gfi",
        gathered_first.astype(jnp.float32),
        gradient_projected,
        precision=PRECISION_MAX,
    )
    grad_normed_one = jnp.einsum(
        "zqtv,btv->zqb",
        gradient_projected,
        input_weight_whole.astype(jnp.float32),
        precision=PRECISION_MAX,
    )
    norm_pull_one = jax.vjp(rms_scale, slot_tokens, norm1_gain)[1]
    grad_tok_norm, grad_gain_one = norm_pull_one(collect_back(grad_normed_one))
    input_slot = (grad_middle + grad_tok_norm).astype(jnp.bfloat16)
    grad_in, grad_out, grad_gate_up, grad_down = (
        lax.psum_scatter(
            grad_in.astype(jnp.bfloat16), "fsdp", scatter_dimension=0, tiled=True
        ).astype(jnp.float32),
        lax.psum_scatter(
            grad_out.astype(jnp.bfloat16), "fsdp", scatter_dimension=1, tiled=True
        ).astype(jnp.float32),
        lax.psum_scatter(
            grad_gate_up.astype(jnp.bfloat16), "fsdp", scatter_dimension=0, tiled=True
        ).astype(jnp.float32),
        lax.psum_scatter(
            grad_down.astype(jnp.bfloat16), "fsdp", scatter_dimension=1, tiled=True
        ).astype(jnp.float32),
    )
    conv_full = lax.dynamic_update_slice_in_dim(jnp.zeros_like(conv_w), grad_conv, head_start, 0)
    log_full = lax.dynamic_update_slice_in_dim(jnp.zeros_like(decay_log), grad_log, head_start, 0)
    bias_full = lax.dynamic_update_slice_in_dim(
        jnp.zeros_like(decay_bias), grad_bias, head_start, 0
    )
    small_sums = lax.psum(
        (grad_gain_one, grad_gain_two, conv_full, log_full, bias_full, grad_gain_out),
        ("fsdp", "tp"),
    )
    out_home = jnp.einsum(
        "sg,std->gtd", take_pick, block_out.astype(jnp.bfloat16), preferred_element_type=jnp.float32
    ).astype(jnp.bfloat16)
    grad_home = jnp.einsum(
        "sg,std->gtd", take_pick, input_slot, preferred_element_type=jnp.float32
    ).astype(jnp.bfloat16)
    back_out, back_grad = (
        lax.all_to_all(out_home, "fsdp", split_axis=0, concat_axis=0, tiled=True),
        lax.all_to_all(grad_home, "fsdp", split_axis=0, concat_axis=0, tiled=True),
    )
    output = jnp.einsum(
        "gj,gtd->jtd", send_pick, back_out, preferred_element_type=jnp.float32
    ).astype(jnp.bfloat16)
    input_grad = jnp.einsum(
        "gj,gtd->jtd", send_pick, back_grad, preferred_element_type=jnp.float32
    ).astype(jnp.bfloat16)
    return (
        output,
        input_grad,
        small_sums[0],
        grad_in,
        small_sums[2],
        small_sums[3],
        small_sums[4],
        small_sums[5],
        grad_out,
        small_sums[1],
        grad_gate_up,
        grad_down,
    )


def solution(mesh):
    return jax.shard_map(
        local,
        mesh=mesh,
        in_specs=(
            P("fsdp", "tp", None),
            P(),
            P(),
            P("fsdp", "tp", None),
            P(),
            P("fsdp", "tp", None),
            P(),
            P(),
            P(),
            P(),
            P("tp", "fsdp"),
            P(),
            P("fsdp", None, "tp"),
            P("tp", "fsdp"),
        ),
        out_specs=(
            P("fsdp", "tp", None),
            P("fsdp", "tp", None),
            P(),
            P("fsdp", "tp", None),
            P(),
            P(),
            P(),
            P(),
            P("tp", "fsdp"),
            P(),
            P("fsdp", None, "tp"),
            P("tp", "fsdp"),
        ),
        check_vma=False,
    )
```

profile of v0, /device:TPU:8, one launch (start us, length us, event | category | flops | bytes accessed | tf_op | source)
XLA Modules:
  0.0 2863.2 jit_solution(13583249474675545995)
XLA Ops:
  22.7 57.9 %all-to-all-done = bf16[8,256,1024]{2,1,0:T(8,128)(2,1)} async-done(((bf16[8,256,1024]{2,1,0:T(8,128)(2,1)}), bf16[8,256,1024]{2,1,0:T(8,128)(2,1)}, u32[]{:S(2)}, u32[]{:S(2)}) %all-to-all-start) | async-done | bytes 4194336 | tf_op jit(solution)/shard_map/all_to_all | solution.py:181
  99.7 65.8 %all-gather.8.cloned.1.call-done = bf16[2,1024,1024]{2,0,1:T(2,128)(2,1)} async-done(((bf16[2,256,1024]{2,0,1:T(2,128)(2,1)}), bf16[2,1024,1024]{2,0,1:T(2,128)(2,1)}) %all-gather.8.cloned.1.call-update) | async-done | bytes 4194320 | tf_op jit(solution)/shard_map/all_gather | solution.py:130
  263.2 630.3 %custom-call.10 = f32[16,2,2,1,128,128]{4,5,3,2,1,0:T(8,128)} custom-call(f32[16,2,2,1,128,128]{5,4,3,2,1,0:T(8,128)} %get-tuple-element.727), custom_call_target="InvertDiagBlocksLowerTriangular" | custom-call | tf_op jit(solution)/shard_map/jvp(jit(_solve_triangular))/vmap(vmap(vmap()))/triangular_solve | solution.py:77
  925.0 81.9 %while.38 = (s32[]{:T(128)}, f32[2,2,128,128]{3,2,1,0:T(8,128)S(1)}, f32[16,2,2,128,128]{4,3,2,1,0:T(8,128)}, f32[16,2,2,128,128]{4,3,2,1,0:T(8,128)}, f32[16,2,...) while((s32[]{:T(128)}, ...), condition=%wide.region_6.7_spmd.clone, body=%wide.region_5.6_spmd.clone.sunk | while | flops 201719808 | bytes 2885797 | solution.py:86
  1059.3 152.3 %all-reduce.36.cloned.1.call-done = bf16[2,1024,1024]{2,0,1:T(2,128)(2,1)} async-done(((bf16[2,1024,1024]{2,0,1:T(2,128)(2,1)}), bf16[2,1024,1024]{2,0,1:T(2,128)(2,1)}) %all-reduce.36.cloned.1.call-update) | async-done | bytes 4194320
  1222.7 23.7 all-gather.14.cloned.1.call-done
  1246.4 80.2 %all-gather.12.cloned.1.call-done = bf16[2,1024,1024]{2,0,1:T(2,128)(2,1)} async-done(((bf16[2,256,1024]{2,0,1:T(2,128)(2,1)}), bf16[2,1024,1024]{2,0,1:T(2,128)(2,1)}) %all-gather.12.cloned.1.call-update) | async-done | bytes 4194320 | tf_op jit(solution)/shard_map/all_gather | solution.py:130
  1355.0 80.4 %all-gather.18.cloned.1.call-done = bf16[2,1024,1024]{2,0,1:T(2,128)(2,1)} async-done(((bf16[2,256,1024]{2,0,1:T(2,128)(2,1)}), bf16[2,1024,1024]{2,0,1:T(2,128)(2,1)}) %all-gather.18.cloned.1.call-update) | async-done | bytes 4194320 | tf_op jit(solution)/shard_map/all_gather | solution.py:140
  1451.0 22.6 bitcast_convert_fusion.1
  1482.2 154.1 %all-reduce.38.cloned.1.call-done = bf16[2,1024,1024]{2,0,1:T(2,128)(2,1)} async-done(((bf16[2,1024,1024]{2,0,1:T(2,128)(2,1)}), bf16[2,1024,1024]{2,0,1:T(2,128)(2,1)}) %all-reduce.38.cloned.1.call-update) | async-done | bytes 4194320
  1673.8 57.9 %all-gather.20.cloned.1.call-done = bf16[2,1024,1024]{2,0,1:T(2,128)(2,1)} async-done(((bf16[2,256,1024]{2,0,1:T(2,128)(2,1)}), bf16[2,1024,1024]{2,0,1:T(2,128)(2,1)}) %all-gather.20.cloned.1.call-update) | async-done | bytes 4194320 | tf_op jit(solution)/shard_map/all_gather | solution.py:140
  1786.2 164.6 %while.39 = (s32[]{:T(128)}, f32[2,2,128,128]{3,2,1,0:T(8,128)S(1)}, f32[16,2,2,128,128]{4,3,2,1,0:T(8,128)}, f32[16,2,2,128,128]{4,3,2,1,0:T(8,128)}, f32[16,2,...) while((s32[]{:T(128)}, ...), condition=%wide.region_19.20_spmd.clone, body=%wide.region_17.19_spmd.clone.sunk | while | flops 403439616 | bytes 4726519 | solution.py:86
  1950.7 16.3 fusion.48
  1979.5 19.7 multiply_reduce_fusion.6
  2120.1 23.4 multiply_reduce_fusion.2
  2177.9 26.0 bitcast_convert_fusion
  2218.2 25.0 bitcast_convert_fusion.4
  2248.0 252.9 %all-reduce.40.cloned.1.call-done = (bf16[2,1024,1024]{2,0,1:T(2,128)(2,1)}, bf16[2,1024,1024]{2,0,1:T(2,128)(2,1)}) async-done(((bf16[2,1024,1024]{2,0,1:T(2,128)(2,1)}, bf16[2,1024,1024]{2,0,1:T(2,128)(2,1)}), (bf16[2,1024,1024]{2,0,1:T(2,128)(2,1)}, bf16[2,1024,1024]{2,0,1:T(2,128)(2,1)})) %all-reduce.40.cloned.1.call-update) | async-done | bytes 8388624
  2524.3 30.6 %bitcast_convert_fusion.3 = bf16[1024,2,771]{0,2,1:T(8,128)(2,1)} fusion(f32[2,1024,2,640]{1,3,2,0:T(8,128)} %copy-done.27, f32[2,1024,2,128]{1,3,2,0:T(8,128)} %get-tuple-element.701, f32[2,1024,2,2]{1,3,2,0:T(2,128)S(1)} %fusion.193, f32[2,1024,2,1]{1,3,2,0:T(1,128)S(1)} %get-tuple-element.703, bf16[2,1024,1024]{2,0,1:T(2,128)(2,1)} %all-gather.8.cloned.1.call-done), kind=kOutput, calls=%fused_computation.85 | convolution fusion | flops 38816751616 | bytes 19984384 | tf_op jit(solution)/shard_map/bwg,bwfi->gfi/dot_general | solution.py:259
  2581.2 56.3 %reduce-scatter.17.cloned.1.call-done = bf16[128,1408]{1,0:T(8,128)(2,1)} async-done(((bf16[1024,1408]{1,0:T(8,128)(2,1)}), bf16[128,1408]{1,0:T(8,128)(2,1)}) %reduce-scatter.17.cloned.1.call-update) | async-done | bytes 360464
  2641.2 33.5 %reduce-scatter.15.cloned.1.call-done = bf16[128,256]{1,0:T(8,128)(2,1)} async-done(((bf16[1024,256]{1,0:T(8,128)(2,1)}), bf16[128,256]{1,0:T(8,128)(2,1)}) %reduce-scatter.15.cloned.1.call-update) | async-done | bytes 65552
  2676.4 49.2 %reduce-scatter.13.cloned.1.call-done = bf16[128,1542]{1,0:T(8,128)(2,1)} async-done(((bf16[1024,1542]{1,0:T(8,128)(2,1)}), bf16[128,1542]{1,0:T(8,128)(2,1)}) %reduce-scatter.13.cloned.1.call-update) | async-done | bytes 394768
  2728.9 39.5 %all-reduce.27 = (f32[1024]{0:T(1024)}, f32[8]{0:T(128)}, f32[8]{0:T(128)}, f32[128]{0:T(128)}, f32[1024]{0:T(1024)}) all-reduce(f32[1024]{0:T(1024)S(1)} %get-tuple-element.632, f32[8]{0:T(128)S(1)} %multiply_dynamic-update-slice_fusion, f32[8]{0:T(128)S(1)} %dynamic_update_slice.55, ...), channel_id=1, replica_groups=mesh['fsdp'=8,'tp'=4] {'fsdp','tp'}, use_global_device_ids=true, to_apply=%region_33.34 | all-reduce | flops 2192 | bytes 17536 | tf_op jit(solution)/shard_map/psum | solution.py:293
  2780.9 74.0 %all-reduce.34.cloned.1.call-done = f32[8,640,4]{1,2,0:T(4,128)} async-done(((f32[8,640,4]{1,2,0:T(4,128)}), f32[8,640,4]{1,2,0:T(4,128)}) %all-reduce.34.cloned.1.call-update) | async-done | bytes 81936 | tf_op jit(solution)/shard_map/psum | solution.py:293
  (641 shorter events, 874.5 us)
Async XLA Ops:
  7.2 92.5 %all-gather.10.cloned.1.call-start = ((), (), s32[]{:S(2)}) async-start(), calls=%async_computation.8 | async-start | bytes 3575808 | tf_op jit(solution)/shard_map/all_gather | solution.py:194
  16.7 63.9 %all-to-all-start = ((bf16[8,256,1024]{2,1,0:T(8,128)(2,1)}), bf16[8,256,1024]{2,1,0:T(8,128)(2,1)}, u32[]{:S(2)}, u32[]{:S(2)}) async-start(bf16[8,256,1024]{2,1,0:T(8,128)(2,1)} %copy.605), calls=%async_computation | async-start | bytes 8388608 | tf_op jit(solution)/shard_map/all_to_all | solution.py:181
  21.4 144.1 %all-gather.8.cloned.1.call-start = ((), (), s32[]{:S(2)}) async-start(), calls=%async_computation.7 | async-start | bytes 5242880 | tf_op jit(solution)/shard_map/all_gather | solution.py:130
  88.0 1123.6 %all-reduce.36.cloned.1.call-start = ((), (), s32[]{:S(2)}) async-start(), calls=%async_computation.19 | async-start | bytes 8388608
  205.8 713.6 %copy-start.81 = (f32[16,2,2,1]{0,2,3,1:T(2,128)}, f32[16,2,2,1]{0,2,3,1:T(2,128)S(1)}, u32[]{:S(2)}) copy-start(f32[16,2,2,1]{0,2,3,1:T(2,128)S(1)} %copy.768) | copy-start | bytes 772
  207.7 799.3 %copy-start.54 = (f32[2,1024,2]{1,2,0:T(2,128)}, f32[2,1024,2]{1,2,0:T(2,128)S(1)}, u32[]{:S(2)}) copy-start(f32[2,1024,2]{1,2,0:T(2,128)S(1)} %multiply_reduce_fusion.14) | copy-start | bytes 49156
  208.6 820.7 %copy-start.39 = (f32[16,2,2,64]{0,2,3,1:T(2,128)}, f32[16,2,2,64]{0,2,3,1:T(2,128)S(1)}, u32[]{:S(2)}) copy-start(f32[16,2,2,64]{0,2,3,1:T(2,128)S(1)} %copy.614) | copy-start | bytes 49156
  255.0 638.7 %copy-start.28 = (f32[2,16,64,2,2]{1,4,2,3,0:T(2,128)}, f32[2,16,64,2,2]{1,4,2,3,0:T(2,128)S(1)}, u32[]{:S(2)}) copy-start(f32[2,16,64,2,2]{1,4,2,3,0:T(2,128)S(1)} %copy.626) | copy-start | bytes 98308
  1057.5 188.9 %all-gather.14.cloned.1.call-start = ((), (), s32[]{:S(2)}) async-start(), calls=%async_computation.10 | async-start | bytes 3244032 | tf_op jit(solution)/shard_map/all_gather | solution.py:213
  1058.0 268.5 %all-gather.12.cloned.1.call-start = ((), (), s32[]{:S(2)}) async-start(), calls=%async_computation.9 | async-start | bytes 5242880 | tf_op jit(solution)/shard_map/all_gather | solution.py:130
  1214.9 430.2 %copy-start.9 = (f32[2,256,1024]{2,0,1:T(2,128)}, f32[2,256,1024]{2,0,1:T(2,128)S(1)}, u32[]{:S(2)}) copy-start(f32[2,256,1024]{2,0,1:T(2,128)S(1)} %get-tuple-element.692) | copy-start | bytes 6291460
  1217.1 137.9 %all-gather.16.cloned.1.call-start = ((), (), s32[]{:S(2)}) async-start(), calls=%async_computation.11 | async-start | bytes 1622016 | tf_op jit(solution)/shard_map/all_gather | solution.py:214
  1217.7 217.7 %all-gather.18.cloned.1.call-start = ((), (), s32[]{:S(2)}) async-start(), calls=%async_computation.12 | async-start | bytes 5242880 | tf_op jit(solution)/shard_map/all_gather | solution.py:140
  1219.9 425.3 %copy-start.35 = (f32[2,256]{0,1:T(8,128)}, f32[2,256]{0,1:T(8,128)S(1)}, u32[]{:S(2)}) copy-start(f32[2,256]{0,1:T(8,128)S(1)} %copy.603) | copy-start | bytes 6148
  1222.6 413.6 %all-reduce.38.cloned.1.call-start = ((), (), s32[]{:S(2)}) async-start(), calls=%async_computation.20 | async-start | bytes 8388608
  1482.1 249.5 %all-gather.20.cloned.1.call-start = ((), (), s32[]{:S(2)}) async-start(), calls=%async_computation.13 | async-start | bytes 5242880 | tf_op jit(solution)/shard_map/all_gather | solution.py:140
  1652.2 848.7 %all-reduce.40.cloned.1.call-start = ((), (), s32[]{:S(2)}) async-start(), calls=%async_computation.21 | async-start | bytes 16777216
  2210.2 369.1 %reduce-scatter.19.cloned.1.call-start = ((), (), s32[]{:S(2)}) async-start(), calls=%async_computation.18 | async-start | bytes 1769472
  2218.1 419.4 %reduce-scatter.17.cloned.1.call-start = ((), (), s32[]{:S(2)}) async-start(), calls=%async_computation.17 | async-start | bytes 3244032
  2514.4 60.2 %all-to-all-start.2 = ((bf16[8,256,1024]{2,1,0:T(8,128)(2,1)}), bf16[8,256,1024]{2,1,0:T(8,128)(2,1)}, u32[]{:S(2)}, u32[]{:S(2)}) async-start(bf16[8,256,1024]{2,1,0:T(8,128)(2,1)} %copy.709), calls=%async_computation.2 | async-start | bytes 8388608 | tf_op jit(solution)/shard_map/all_to_all | solution.py:305
  2519.2 155.6 %reduce-scatter.15.cloned.1.call-start = ((), (), s32[]{:S(2)}) async-start(), calls=%async_computation.16 | async-start | bytes 589824
  2524.1 201.5 %reduce-scatter.13.cloned.1.call-start = ((), (), s32[]{:S(2)}) async-start(), calls=%async_computation.15 | async-start | bytes 3833856
  2574.6 198.8 %all-to-all-start.1 = ((bf16[8,256,1024]{2,1,0:T(8,128)(2,1)}), bf16[8,256,1024]{2,1,0:T(8,128)(2,1)}, u32[]{:S(2)}, u32[]{:S(2)}) async-start(bf16[8,256,1024]{2,1,0:T(8,128)(2,1)} %copy.650), calls=%async_computation.1 | async-start | bytes 8388608 | tf_op jit(solution)/shard_map/all_to_all | solution.py:304
  2579.3 275.6 %all-reduce.34.cloned.1.call-start = ((), (), s32[]{:S(2)}) async-start(), calls=%async_computation.14 | async-start | bytes 163840 | tf_op jit(solution)/shard_map/psum | solution.py:293
  (100 other events, 4151.1 us)
Sparse Core Ops, SparseCore 0:
  10.5 58.4 all-gather.9
  88.2 77.3 all-gather.7
  1057.6 153.9 all-reduce.35
  1213.5 32.8 all-gather.13
  1248.4 78.1 all-gather.11
  1328.5 26.4 all-gather.15
  1357.2 78.1 all-gather.17
  1482.2 153.9 all-reduce.37
  1652.3 79.2 all-gather.19
  2210.3 290.5 all-reduce.39
  2504.2 51.8 reduce-scatter.18
  2559.3 78.1 reduce-scatter.16
  2641.5 33.2 reduce-scatter.14
  2678.1 47.4 reduce-scatter.12
  2732.5 122.3 all-reduce.33
where the time goes:
time: 2880 us; the launch traced here: 2860 us
  waiting for transfers between devices  1160 us (40%)
  other arithmetic  816 us (28%)
  matrix products  569 us (20%)
  local copies, waits for them, and re-layouts  238 us (8%)
  blocking collectives  49.6 us (2%)
    unnamed x22, waiting for transfers between devices  700 us
    another operation x4, other arithmetic, delta_product(): jax.scipy.linalg.solve_triangular(lower_mat, right_sides, lower=True, uni...  638 us
    all_gather x2, waiting for transfers between devices, spread(): return lax.all_gather(value, 'tp', axis=1, tiled=True)  146 us
    all_gather x2, waiting for transfers between devices, spread_back(): return lax.all_gather(value, 'tp', axis=1, tiled=True)  138 us
    dot_general x48, matrix products, carry_step(): jnp.einsum('shid,shdv->shiv', key_block, state, precision=PRECISION_MAX)  98.7 us
    dot_general x48, matrix products, carry_step(): jnp.einsum('shjd,shjv->shdv', weighted_block, updates, precision=PRECISIO...  96.4 us
    psum x1, waiting for transfers between devices, local(): lax.psum((grad_gain_one, grad_gain_two, conv_full, log_full, bias_full, g...  74 us
    all_to_all x1, waiting for transfers between devices, local(): lax.all_to_all(sending, 'fsdp', split_axis=0, concat_axis=0, tiled=True)  57.9 us
  transfers between devices with their start and end apart: 18, of which 15 were waited for; matrix products, arithmetic and copies ran while one was open for 7% of the time, Pallas kernels for 0%

commit v1 on v0

--- a/solution.py
+++ b/solution.py
@@ -1,3 +1,4 @@
+import functools
 import jax
 import jax.numpy as jnp
 from jax import lax
@@ -9,6 +10,16 @@
 EPS_NORM = 1e-05
 EPS_UNIT = 1e-06
 PRECISION_MAX = lax.Precision.HIGHEST
+
+
+def lay_scenes_all(in_array, axis_name, along_dim):
+    parts_out = lax.axis_size(axis_name)
+    local_now = jnp.stack([in_array] * parts_out, axis=0)
+    small = lax.all_to_all(local_now, axis_name, 0, 0)
+    return jnp.concatenate(small, along_dim)
+
+
+review_panels_over_axis = functools.partial(lay_scenes_all, axis_name="tp", along_dim=1)
 
 
 def rms_scale(value, gain):
@@ -127,7 +138,7 @@
 
 
 def spread(value):
-    return lax.all_gather(value, "tp", axis=1, tiled=True)
+    return review_panels_over_axis(value)
 
 
 def collect(value):

time: 2880 us -> 2830 us (0.983)
  waiting for transfers between devices: 1160 us -> 1110 us
    all_to_all x0 -> x2, waiting for transfers between devices: none -> 216 us  [lay_scenes_all(): small = lax.all_to_all(local_now, axis_name, 0, 0)]
    all_gather x2 -> x0, waiting for transfers between devices: 146 us -> none  [spread(): return lax.all_gather(value, 'tp', axis=1, tiled=True)]
    all_gather x2, waiting for transfers between devices: 138 us -> 57.9 us  [spread_back(): return lax.all_gather(value, 'tp', axis=1, tiled=True)]
    unnamed x22 -> x20, waiting for transfers between devices: 700 us -> 704 us
  transfers between devices with their start and end apart: 18 -> 18, of which waited for: 15 -> 12; matrix products, arithmetic and copies ran while one was open for 7% -> 6% of each run, Pallas kernels for 0% -> 0%
where the time goes in v1:
time: 2830 us; the launch traced here: 2820 us
  waiting for transfers between devices  1110 us (39%)
  other arithmetic  811 us (29%)
  matrix products  560 us (20%)
  local copies, waits for them, and re-layouts  243 us (9%)
  blocking collectives  49.6 us (2%)
  starting transfers between devices  28.3 us (1%)
    unnamed x20, waiting for transfers between devices  704 us
    another operation x4, other arithmetic, delta_product(): jax.scipy.linalg.solve_triangular(lower_mat, right_sides, lower=True, uni...  638 us
    all_to_all x2, waiting for transfers between devices, lay_scenes_all(): small = lax.all_to_all(local_now, axis_name, 0, 0)  216 us
    dot_general x48, matrix products, carry_step(): jnp.einsum('shid,shdv->shiv', key_block, state, precision=PRECISION_MAX)  98.8 us
    dot_general x48, matrix products, carry_step(): jnp.einsum('shjd,shjv->shdv', weighted_block, updates, precision=PRECISIO...  96.4 us
    psum x1, waiting for transfers between devices, local(): lax.psum((grad_gain_one, grad_gain_two, conv_full, log_full, bias_full, g...  74.1 us
    all_gather x2, waiting for transfers between devices, spread_back(): return lax.all_gather(value, 'tp', axis=1, tiled=True)  57.9 us
  transfers between devices with their start and end apart: 18, of which 12 were waited for; matrix products, arithmetic and copies ran while one was open for 6% of the time, Pallas kernels for 0%

profile of v1, /device:TPU:8, one launch (start us, length us, event | category | flops | bytes accessed | tf_op | source)
XLA Modules:
  0.0 2817.3 jit_solution(14211982804223610890)
XLA Ops:
  20.2 48.4 %all-to-all-done = bf16[8,256,1024]{2,1,0:T(8,128)(2,1)} async-done(((bf16[8,256,1024]{2,1,0:T(8,128)(2,1)}), bf16[8,256,1024]{2,1,0:T(8,128)(2,1)}, u32[]{:S(2)}, u32[]{:S(2)}) %all-to-all-start) | async-done | bytes 4194336 | tf_op jit(solution)/shard_map/all_to_all | solution.py:192
  96.2 74.6 %all-to-all-done.1 = bf16[4,2,256,1024]{3,2,1,0:T(8,128)(2,1)} async-done(((bf16[4,2,256,1024]{3,2,1,0:T(8,128)(2,1)}), bf16[4,2,256,1024]{3,2,1,0:T(8,128)(2,1)}, u32[]{:S(2)}, u32[]{:S(2)}) %all-to-all-start.1) | async-done | bytes 4194336 | tf_op jit(solution)/shard_map/all_to_all | solution.py:18
  198.1 19.8 fusion.39
  288.0 630.3 %custom-call.10 = f32[16,2,2,1,128,128]{4,5,3,2,1,0:T(8,128)} custom-call(f32[16,2,2,1,128,128]{5,4,3,2,1,0:T(8,128)} %get-tuple-element.725), custom_call_target="InvertDiagBlocksLowerTriangular" | custom-call | tf_op jit(solution)/shard_map/jvp(jit(_solve_triangular))/vmap(vmap(vmap()))/triangular_solve | solution.py:88
  947.9 71.1 %while.38 = (s32[]{:T(128)}, f32[2,2,128,128]{3,2,1,0:T(8,128)S(1)}, f32[16,2,2,128,128]{4,3,2,1,0:T(8,128)}, f32[16,2,2,128,128]{4,3,2,1,0:T(8,128)}, f32[16,2,...) while((s32[]{:T(128)}, ...), condition=%wide.region_6.7_spmd.clone, body=%wide.region_5.6_spmd.clone.sunk | while | flops 201719808 | bytes 2885797 | solution.py:97
  1075.4 153.6 %all-reduce.36.cloned.1.call-done = bf16[2,1024,1024]{2,0,1:T(2,128)(2,1)} async-done(((bf16[2,1024,1024]{2,0,1:T(2,128)(2,1)}), bf16[2,1024,1024]{2,0,1:T(2,128)(2,1)}) %all-reduce.36.cloned.1.call-update) | async-done | bytes 4194320
  1246.8 141.1 %all-to-all-done.2 = bf16[4,2,256,1024]{3,2,1,0:T(8,128)(2,1)} async-done(((bf16[4,2,256,1024]{3,2,1,0:T(8,128)(2,1)}), bf16[4,2,256,1024]{3,2,1,0:T(8,128)(2,1)}, u32[]{:S(2)}, u32[]{:S(2)}) %all-to-all-start.2) | async-done | bytes 4194336 | tf_op jit(solution)/shard_map/all_to_all | solution.py:18
  1419.8 22.7 bitcast_convert_fusion.1
  1451.1 155.4 %all-reduce.38.cloned.1.call-done = bf16[2,1024,1024]{2,0,1:T(2,128)(2,1)} async-done(((bf16[2,1024,1024]{2,0,1:T(2,128)(2,1)}), bf16[2,1024,1024]{2,0,1:T(2,128)(2,1)}) %all-reduce.38.cloned.1.call-update) | async-done | bytes 4194320
  1635.5 57.9 %all-gather.14.cloned.1.call-done = bf16[2,1024,1024]{2,0,1:T(2,128)(2,1)} async-done(((bf16[2,256,1024]{2,0,1:T(2,128)(2,1)}), bf16[2,1024,1024]{2,0,1:T(2,128)(2,1)}) %all-gather.14.cloned.1.call-update) | async-done | bytes 4194320 | tf_op jit(solution)/shard_map/all_gather | solution.py:151
  1747.8 153.8 %while.39 = (s32[]{:T(128)}, f32[2,2,128,128]{3,2,1,0:T(8,128)S(1)}, f32[16,2,2,128,128]{4,3,2,1,0:T(8,128)}, f32[16,2,2,128,128]{4,3,2,1,0:T(8,128)}, f32[16,2,...) while((s32[]{:T(128)}, ...), condition=%wide.region_19.20_spmd.clone, body=%wide.region_17.19_spmd.clone.sunk | while | flops 403439616 | bytes 4726519 | solution.py:97
  1901.6 16.4 fusion.48
  1930.4 19.8 multiply_reduce_fusion.6
  2071.8 24.4 multiply_reduce_fusion.2
  2110.8 16.2 pad_add_fusion.2
  2130.8 25.9 bitcast_convert_fusion
  2171.0 23.0 bitcast_convert_fusion.4
  2198.7 255.1 %all-reduce.40.cloned.1.call-done = (bf16[2,1024,1024]{2,0,1:T(2,128)(2,1)}, bf16[2,1024,1024]{2,0,1:T(2,128)(2,1)}) async-done(((bf16[2,1024,1024]{2,0,1:T(2,128)(2,1)}, bf16[2,1024,1024]{2,0,1:T(2,128)(2,1)}), (bf16[2,1024,1024]{2,0,1:T(2,128)(2,1)}, bf16[2,1024,1024]{2,0,1:T(2,128)(2,1)})) %all-reduce.40.cloned.1.call-update) | async-done | bytes 8388624
  2478.0 27.3 bitcast_convert_fusion.3
  2535.3 56.1 %reduce-scatter.17.cloned.1.call-done = bf16[128,1408]{1,0:T(8,128)(2,1)} async-done(((bf16[1024,1408]{1,0:T(8,128)(2,1)}), bf16[128,1408]{1,0:T(8,128)(2,1)}) %reduce-scatter.17.cloned.1.call-update) | async-done | bytes 360464
  2594.9 33.7 %reduce-scatter.15.cloned.1.call-done = bf16[128,256]{1,0:T(8,128)(2,1)} async-done(((bf16[1024,256]{1,0:T(8,128)(2,1)}), bf16[128,256]{1,0:T(8,128)(2,1)}) %reduce-scatter.15.cloned.1.call-update) | async-done | bytes 65552
  2630.3 49.2 %reduce-scatter.13.cloned.1.call-done = bf16[128,1542]{1,0:T(8,128)(2,1)} async-done(((bf16[1024,1542]{1,0:T(8,128)(2,1)}), bf16[128,1542]{1,0:T(8,128)(2,1)}) %reduce-scatter.13.cloned.1.call-update) | async-done | bytes 394768
  2682.8 39.5 %all-reduce.27 = (f32[1024]{0:T(1024)}, f32[8]{0:T(128)}, f32[8]{0:T(128)}, f32[128]{0:T(128)}, f32[1024]{0:T(1024)}) all-reduce(f32[1024]{0:T(1024)S(1)} %get-tuple-element.635, f32[8]{0:T(128)S(1)} %multiply_dynamic-update-slice_fusion, f32[8]{0:T(128)S(1)} %dynamic_update_slice.55, ...), channel_id=1, replica_groups=mesh['fsdp'=8,'tp'=4] {'fsdp','tp'}, use_global_device_ids=true, to_apply=%region_33.34 | all-reduce | flops 2192 | bytes 17536 | tf_op jit(solution)/shard_map/psum | solution.py:304
  2734.9 74.1 %all-reduce.34.cloned.1.call-done = f32[8,640,4]{1,2,0:T(4,128)} async-done(((f32[8,640,4]{1,2,0:T(4,128)}), f32[8,640,4]{1,2,0:T(4,128)}) %all-reduce.34.cloned.1.call-update) | async-done | bytes 81936 | tf_op jit(solution)/shard_map/psum | solution.py:304
  (646 shorter events, 835.5 us)
Async XLA Ops:
  14.8 53.8 %all-to-all-start = ((bf16[8,256,1024]{2,1,0:T(8,128)(2,1)}), bf16[8,256,1024]{2,1,0:T(8,128)(2,1)}, u32[]{:S(2)}, u32[]{:S(2)}) async-start(bf16[8,256,1024]{2,1,0:T(8,128)(2,1)} %copy.604), calls=%async_computation | async-start | bytes 8388608 | tf_op jit(solution)/shard_map/all_to_all | solution.py:192
  73.9 1536.7 %copy-start.6 = (f32[2,256,1024]{2,0,1:T(2,128)}, f32[2,256,1024]{2,0,1:T(2,128)S(1)}, u32[]{:S(2)}) copy-start(f32[2,256,1024]{2,0,1:T(2,128)S(1)} %get-tuple-element.732) | copy-start | bytes 6291460
  78.4 92.4 %all-to-all-start.1 = ((bf16[4,2,256,1024]{3,2,1,0:T(8,128)(2,1)}), bf16[4,2,256,1024]{3,2,1,0:T(8,128)(2,1)}, u32[]{:S(2)}, u32[]{:S(2)}) async-start(bf16[4,2,256,1024]{3,2,1,0:T(8,128)(2,1)} %stack.4), calls=%async_computation.1 | async-start | bytes 8388608 | tf_op jit(solution)/shard_map/all_to_all | solution.py:18
  83.9 91.6 %all-gather.6.cloned.1.call-start = ((), (), s32[]{:S(2)}) async-start(), calls=%async_computation.9 | async-start | bytes 3575808 | tf_op jit(solution)/shard_map/all_gather | solution.py:205
  84.7 1144.3 %all-reduce.36.cloned.1.call-start = ((), (), s32[]{:S(2)}) async-start(), calls=%async_computation.19 | async-start | bytes 8388608
  228.9 713.1 %copy-start.84 = (f32[16,2,2,1]{0,2,3,1:T(2,128)}, f32[16,2,2,1]{0,2,3,1:T(2,128)S(1)}, u32[]{:S(2)}) copy-start(f32[16,2,2,1]{0,2,3,1:T(2,128)S(1)} %copy.765) | copy-start | bytes 772
  230.7 788.4 %copy-start.51 = (f32[2,1024,2]{1,2,0:T(2,128)}, f32[2,1024,2]{1,2,0:T(2,128)S(1)}, u32[]{:S(2)}) copy-start(f32[2,1024,2]{1,2,0:T(2,128)S(1)} %multiply_reduce_fusion.14) | copy-start | bytes 49156
  279.8 638.8 %copy-start.30 = (f32[2,16,64,2,2]{1,4,2,3,0:T(2,128)}, f32[2,16,64,2,2]{1,4,2,3,0:T(2,128)S(1)}, u32[]{:S(2)}) copy-start(f32[2,16,64,2,2]{1,4,2,3,0:T(2,128)S(1)} %copy.625) | copy-start | bytes 98308
  1072.9 319.7 %all-gather.8.cloned.1.call-start = ((), (), s32[]{:S(2)}) async-start(), calls=%async_computation.10 | async-start | bytes 3244032 | tf_op jit(solution)/shard_map/all_gather | solution.py:224
  1073.6 330.5 %all-gather.10.cloned.1.call-start = ((), (), s32[]{:S(2)}) async-start(), calls=%async_computation.11 | async-start | bytes 1622016 | tf_op jit(solution)/shard_map/all_gather | solution.py:225
  1231.0 379.6 %copy-start.17 = (bf16[2,256,1024]{2,0,1:T(2,128)(2,1)}, bf16[2,256,1024]{2,0,1:T(2,128)(2,1)S(1)}, u32[]{:S(2)}) copy-start(bf16[2,256,1024]{2,0,1:T(2,128)(2,1)S(1)} %constant_dynamic-slice_fusion.10) | copy-start | bytes 3145732
  1231.9 378.7 %copy-start.66 = (f32[2,256]{1,0:T(2,128)}, f32[2,256]{1,0:T(2,128)S(1)}, u32[]{:S(2)}) copy-start(f32[2,256]{1,0:T(2,128)S(1)} %fusion.201) | copy-start | bytes 6148
  1235.2 152.8 %all-to-all-start.2 = ((bf16[4,2,256,1024]{3,2,1,0:T(8,128)(2,1)}), bf16[4,2,256,1024]{3,2,1,0:T(8,128)(2,1)}, u32[]{:S(2)}, u32[]{:S(2)}) async-start(bf16[4,2,256,1024]{3,2,1,0:T(8,128)(2,1)} %stack.5), calls=%async_computation.2 | async-start | bytes 8388608 | tf_op jit(solution)/shard_map/all_to_all | solution.py:18
  1243.2 160.9 %all-gather.12.cloned.1.call-start = ((), (), s32[]{:S(2)}) async-start(), calls=%async_computation.12 | async-start | bytes 5242880 | tf_op jit(solution)/shard_map/all_gather | solution.py:151
  1246.8 359.7 %all-reduce.38.cloned.1.call-start = ((), (), s32[]{:S(2)}) async-start(), calls=%async_computation.20 | async-start | bytes 8388608
  1451.0 242.3 %all-gather.14.cloned.1.call-start = ((), (), s32[]{:S(2)}) async-start(), calls=%async_computation.13 | async-start | bytes 5242880 | tf_op jit(solution)/shard_map/all_gather | solution.py:151
  1613.9 839.9 %all-reduce.40.cloned.1.call-start = ((), (), s32[]{:S(2)}) async-start(), calls=%async_computation.21 | async-start | bytes 16777216
  2163.1 370.4 %reduce-scatter.19.cloned.1.call-start = ((), (), s32[]{:S(2)}) async-start(), calls=%async_computation.18 | async-start | bytes 1769472
  2171.0 420.4 %reduce-scatter.17.cloned.1.call-start = ((), (), s32[]{:S(2)}) async-start(), calls=%async_computation.17 | async-start | bytes 3244032
  2468.2 60.3 %all-to-all-start.4 = ((bf16[8,256,1024]{2,1,0:T(8,128)(2,1)}), bf16[8,256,1024]{2,1,0:T(8,128)(2,1)}, u32[]{:S(2)}, u32[]{:S(2)}) async-start(bf16[8,256,1024]{2,1,0:T(8,128)(2,1)} %copy.712), calls=%async_computation.4 | async-start | bytes 8388608 | tf_op jit(solution)/shard_map/all_to_all | solution.py:316
  2473.1 155.6 %reduce-scatter.15.cloned.1.call-start = ((), (), s32[]{:S(2)}) async-start(), calls=%async_computation.16 | async-start | bytes 589824
  2478.0 201.5 %reduce-scatter.13.cloned.1.call-start = ((), (), s32[]{:S(2)}) async-start(), calls=%async_computation.15 | async-start | bytes 3833856
  2528.5 198.9 %all-to-all-start.3 = ((bf16[8,256,1024]{2,1,0:T(8,128)(2,1)}), bf16[8,256,1024]{2,1,0:T(8,128)(2,1)}, u32[]{:S(2)}, u32[]{:S(2)}) async-start(bf16[8,256,1024]{2,1,0:T(8,128)(2,1)} %copy.651), calls=%async_computation.3 | async-start | bytes 8388608 | tf_op jit(solution)/shard_map/all_to_all | solution.py:315
  2533.2 275.8 %all-reduce.34.cloned.1.call-start = ((), (), s32[]{:S(2)}) async-start(), calls=%async_computation.14 | async-start | bytes 163840 | tf_op jit(solution)/shard_map/psum | solution.py:304
  (102 other events, 5488.3 us)
Sparse Core Ops, SparseCore 0:
  87.2 32.0 all-gather.5
  1073.0 155.9 all-reduce.35
  1231.1 32.8 all-gather.7
  1265.8 25.2 all-gather.9
  1293.2 107.5 all-gather.11
  1451.2 155.2 all-reduce.37
  1614.1 79.2 all-gather.13
  2163.2 290.5 all-reduce.39
  2457.1 52.8 reduce-scatter.18
  2513.2 78.1 reduce-scatter.16
  2595.4 33.2 reduce-scatter.14
  2632.0 47.4 reduce-scatter.12
  2686.6 122.3 all-reduce.33
